TPU v7x, 512 devices: a whole 4x8x8 slice. The times are simulated.
512 devices in a mesh: vol: 64 (over z_lo, y, core), strip: 8 (over z_hi, x).
Axes of the slice: x: 4, y: 8, z: 8 (z_hi: 2, z_lo: 4; z = z_hi * 4 + z_lo), core: 2. Of those that a mesh axis runs over, the one named last changes fastest.
Arguments:
- frames: bfloat16 [128, 1, 2048, 1024], P('vol', None, 'strip'), may hold values from 0.5 to 4
- kappa: float32 [128], P('vol'), may hold values from 0.3 to 3
Outputs:
- dff: bfloat16 [128, 1, 256, 8, 1024], P(None, None, 'vol', 'strip')
- slope: bfloat16 [128, 1, 256, 8, 1024], P(None, None, 'vol', 'strip')
All inputs are finite; a program needn't handle non-finite values.
Results may differ from a plain program's by a relative error of at most 0.0097.
Values may be sent and summed in bfloat16 or wider, within the bound.
No kernel may reach another device: no remote copies, remote signals or barrier semaphores. Data moves between devices by JAX's collectives and lax.ppermute only.
A program may use at most 64 MiB of HBM per device.

v0:
```python
import jax
import jax.numpy as jnp
from jax import lax
from jax.sharding import PartitionSpec as P

PASSES = 3
BAND = 16


def extended_2(value, sides, width):
    for axis, dim in sides:
        devices, length = (lax.axis_size(axis), value.shape[dim])
        up = [(i, (i + 1) % devices) for i in range(devices - 1)]
        down = [(j, i) for i, j in up]
        last = lax.slice_in_dim(value, length - width, length, axis=dim)
        first = lax.slice_in_dim(value, 0, width, axis=dim)
        before = lax.ppermute(last, axis, up)
        after = lax.ppermute(first, axis, down)
        value = jnp.concatenate([before, value, after], axis=dim)
    return value


def flux(diff, kap):
    ratio = diff / kap
    return diff / (1.0 + ratio * ratio)


def advance(extended, kap):
    center = extended[..., 1:-1, :]
    upper = extended[..., :-2, :] - center
    lower = extended[..., 2:, :] - center
    padded = jnp.pad(center, [(0, 0)] * (center.ndim - 1) + [(1, 1)])
    left = padded[..., :-2] - center
    right = padded[..., 2:] - center
    total = flux(upper, kap) + flux(lower, kap) + flux(left, kap) + flux(right, kap)
    return center + 0.2 * total


def smooth_weights(times):
    steps = jnp.arange(times, dtype=jnp.int32)
    gap = jnp.abs(steps[:, None] - steps[None, :])
    raw = jnp.where(gap <= BAND, BAND + 1 - gap, 0).astype(jnp.float32)
    return (raw / jnp.sum(raw, axis=1, keepdims=True)).astype(jnp.bfloat16)


def detrend(piece):
    times = piece.shape[0]
    weights = smooth_weights(times)
    flat = piece.reshape(times, -1)
    baseline = jnp.dot(weights, flat, preferred_element_type=jnp.float32)
    ratio = (flat.astype(jnp.float32) - baseline) / (baseline + 0.1)
    slope = jnp.concatenate(
        [ratio[1:2] - ratio[0:1], (ratio[2:] - ratio[:-2]) * 0.5, ratio[-1:] - ratio[-2:-1]], axis=0
    )
    return (
        ratio.reshape(piece.shape).astype(jnp.bfloat16),
        slope.reshape(piece.shape).astype(jnp.bfloat16),
    )


def local(frames, kappa):
    kap = kappa[:, None, None, None]
    field = frames.astype(jnp.float32)
    for step in range(PASSES):
        extended = extended_2(field, (("strip", 2),), 1)
        field = advance(extended, kap)
    stored = field.astype(jnp.bfloat16)
    ratio, slope = detrend(lax.all_to_all(stored, "vol", split_axis=2, concat_axis=0, tiled=True))
    return (ratio[:, :, :, None, :], slope[:, :, :, None, :])


def solution(mesh):
    placed = (P("vol", None, "strip", None), P("vol"))
    return jax.shard_map(
        local,
        mesh=mesh,
        in_specs=placed,
        out_specs=(P(None, None, "vol", "strip", None), P(None, None, "vol", "strip", None)),
        check_vma=False,
    )
```

profile of v0, /device:TPU:7, one launch (start us, length us, event | category | flops | bytes accessed | tf_op | source)
XLA Modules:
  0.0 106.4 jit_solution(1144931617588871949)
XLA Ops:
  0.6 0.0 copy-start
  0.6 0.0 copy-start.1
  0.7 0.9 fusion.23
  1.5 10.6 %collective-permute-start = (f32[2,1,1,1024]{3,2,1,0:T(1,128)S(1)}, f32[2,1,1,1024]{3,2,1,0:T(1,128)S(1)}, u32[]{:S(2)}, u32[]{:S(2)}) collective-permute-start(f32[2,1,1,1024]{3,2,1,0:T(1,128)S(1)} %get-tuple-element.20), channel_id=1, source_target_pairs={{0,1},{1,2},{2,3},{3,4},{4,5},{5,6},{6,7},{8,9},{9,10},{10,11},{11... | collective-permute-start | bytes 24584 | tf_op jit(solution)/shard_map/ppermute | solution.py:17
  12.1 1.9 %collective-permute-start.1 = (f32[2,1,1,1024]{3,2,1,0:T(1,128)S(1)}, f32[2,1,1,1024]{3,2,1,0:T(1,128)S(1)}, u32[]{:S(2)}, u32[]{:S(2)}) collective-permute-start(f32[2,1,1,1024]{3,2,1,0:T(1,128)S(1)} %get-tuple-element.21), channel_id=1, source_target_pairs={{1,0},{2,1},{3,2},{4,3},{5,4},{6,5},{7,6},{9,8},{10,9},{11,10},{12... | collective-permute-start | bytes 24584 | tf_op jit(solution)/shard_map/ppermute | solution.py:18
  14.0 1.5 %convert_element_type.49 = f32[2,1,256,1024]{3,2,1,0:T(8,128)S(1)} convert(bf16[2,1,256,1024]{3,2,1,0:T(8,128)(2,1)} %param.2) | non-fusion elementwise | flops 524288 | bytes 3145728 | tf_op jit(solution)/shard_map/convert_element_type | solution.py:63
  15.5 0.0 collective-permute-done
  15.5 7.0 %collective-permute-done.1 = f32[2,1,1,1024]{3,2,1,0:T(1,128)S(1)} collective-permute-done((f32[2,1,1,1024]{3,2,1,0:T(1,128)S(1)}, f32[2,1,1,1024]{3,2,1,0:T(1,128)S(1)}, u32[]{:S(2)}, u32[]{:S(2)}) %collective-permute-start.1) | collective-permute-done | bytes 8224 | tf_op jit(solution)/shard_map/ppermute | solution.py:18
  22.5 0.0 copy-done
  22.5 0.0 copy-done.1
  22.5 2.7 %convert_add_fusion = f32[2,1,256,1024]{3,2,1,0:T(8,128)S(1)} fusion(bf16[2,1,256,1024]{3,2,1,0:T(8,128)(2,1)S(1)} %copy-done, f32[2,1,256,1024]{3,2,1,0:T(8,128)S(1)} %convert_element_type.49, f32[2,1,1,1024]{3,2,1,0:T(1,128)S(1)} %collective-permute-done.1, f32[2,1,1,1024]{3,2,1,0:T(1,128)S(1)} %collective-permute-done, f32[2]{0:T(128)S(1)} %copy-done.1), kind=kLoop, calls=%fused_computation | loop fusion | flops 14680064 | bytes 5259272 | tf_op jit(solution)/shard_map/add | solution.py:36
  25.2 2.4 %collective-permute-start.2 = (f32[2,1,1,1024]{3,2,1,0:T(1,128)S(1)}, f32[2,1,1,1024]{3,2,1,0:T(1,128)S(1)}, u32[]{:S(2)}, u32[]{:S(2)}) collective-permute-start(f32[2,1,1,1024]{3,2,1,0:T(1,128)S(1)} %get-tuple-element.18), channel_id=1, source_target_pairs={{0,1},{1,2},{2,3},{3,4},{4,5},{5,6},{6,7},{8,9},{9,10},{10,11},{11... | collective-permute-start | bytes 24584 | tf_op jit(solution)/shard_map/ppermute | solution.py:17
  27.7 2.9 %collective-permute-start.3 = (f32[2,1,1,1024]{3,2,1,0:T(1,128)S(1)}, f32[2,1,1,1024]{3,2,1,0:T(1,128)S(1)}, u32[]{:S(2)}, u32[]{:S(2)}) collective-permute-start(f32[2,1,1,1024]{3,2,1,0:T(1,128)S(1)} %get-tuple-element.19), channel_id=1, source_target_pairs={{1,0},{2,1},{3,2},{4,3},{5,4},{6,5},{7,6},{9,8},{10,9},{11,10},{12... | collective-permute-start | bytes 24584 | tf_op jit(solution)/shard_map/ppermute | solution.py:18
  30.5 0.0 collective-permute-done.2
  30.5 7.5 %collective-permute-done.3 = f32[2,1,1,1024]{3,2,1,0:T(1,128)S(1)} collective-permute-done((f32[2,1,1,1024]{3,2,1,0:T(1,128)S(1)}, f32[2,1,1,1024]{3,2,1,0:T(1,128)S(1)}, u32[]{:S(2)}, u32[]{:S(2)}) %collective-permute-start.3) | collective-permute-done | bytes 8224 | tf_op jit(solution)/shard_map/ppermute | solution.py:18
  38.1 2.6 %multiply_add_fusion = f32[2,1,256,1024]{3,2,1,0:T(8,128)S(1)} fusion(f32[2,1,256,1024]{3,2,1,0:T(8,128)S(1)} %convert_add_fusion, f32[2,1,1,1024]{3,2,1,0:T(1,128)S(1)} %collective-permute-done.3, f32[2,1,1,1024]{3,2,1,0:T(1,128)S(1)} %collective-permute-done.2, f32[2]{0:T(128)S(1)} %copy-done.1), kind=kLoop, calls=%fused_computation.30 | loop fusion | flops 14155776 | bytes 4210696 | tf_op jit(solution)/shard_map/add | solution.py:36
  40.7 1.9 %collective-permute-start.4 = (f32[2,1,1,1024]{3,2,1,0:T(1,128)S(1)}, f32[2,1,1,1024]{3,2,1,0:T(1,128)S(1)}, u32[]{:S(2)}, u32[]{:S(2)}) collective-permute-start(f32[2,1,1,1024]{3,2,1,0:T(1,128)S(1)} %get-tuple-element.16), channel_id=1, source_target_pairs={{0,1},{1,2},{2,3},{3,4},{4,5},{5,6},{6,7},{8,9},{9,10},{10,11},{11... | collective-permute-start | bytes 24584 | tf_op jit(solution)/shard_map/ppermute | solution.py:17
  42.7 3.4 %collective-permute-start.5 = (f32[2,1,1,1024]{3,2,1,0:T(1,128)S(1)}, f32[2,1,1,1024]{3,2,1,0:T(1,128)S(1)}, u32[]{:S(2)}, u32[]{:S(2)}) collective-permute-start(f32[2,1,1,1024]{3,2,1,0:T(1,128)S(1)} %get-tuple-element.17), channel_id=1, source_target_pairs={{1,0},{2,1},{3,2},{4,3},{5,4},{6,5},{7,6},{9,8},{10,9},{11,10},{12... | collective-permute-start | bytes 24584 | tf_op jit(solution)/shard_map/ppermute | solution.py:18
  46.0 0.0 collective-permute-done.4
  46.1 7.0 %collective-permute-done.5 = f32[2,1,1,1024]{3,2,1,0:T(1,128)S(1)} collective-permute-done((f32[2,1,1,1024]{3,2,1,0:T(1,128)S(1)}, f32[2,1,1,1024]{3,2,1,0:T(1,128)S(1)}, u32[]{:S(2)}, u32[]{:S(2)}) %collective-permute-start.5) | collective-permute-done | bytes 8224 | tf_op jit(solution)/shard_map/ppermute | solution.py:18
  53.1 2.7 %add_convert_fusion = bf16[2,1,256,1024]{3,2,1,0:T(8,128)(2,1)S(1)} fusion(f32[2,1,256,1024]{3,2,1,0:T(8,128)S(1)} %multiply_add_fusion, f32[2,1,1,1024]{3,2,1,0:T(1,128)S(1)} %collective-permute-done.5, f32[2,1,1,1024]{3,2,1,0:T(1,128)S(1)} %collective-permute-done.4, f32[2]{0:T(128)S(1)} %copy-done.1), kind=kLoop, calls=%fused_computation.29 | loop fusion | flops 14680064 | bytes 3162120 | tf_op jit(solution)/shard_map/convert_element_type | solution.py:67
  55.8 2.0 %copy.41 = bf16[2,1,256,1024]{3,0,1,2:T(2,128)(2,1)} copy(bf16[2,1,256,1024]{3,2,1,0:T(8,128)(2,1)S(1)} %add_convert_fusion) | data formatting | bytes 2097152 | tf_op jit(solution)/shard_map/convert_element_type | solution.py:67
  57.8 14.3 %all-to-all-start = ((bf16[2,1,256,1024]{3,0,1,2:T(2,128)(2,1)}), bf16[2,1,256,1024]{3,0,1,2:T(2,128)(2,1)S(1)}, u32[]{:S(2)}, u32[]{:S(2)}) async-start(bf16[2,1,256,1024]{3,0,1,2:T(2,128)(2,1)} %copy.41), calls=%async_computation | async-start | bytes 2097152 | tf_op jit(solution)/shard_map/all_to_all | solution.py:68
  72.1 0.1 convert_reduce_fusion
  72.3 28.7 %all-to-all-done = bf16[2,1,256,1024]{3,0,1,2:T(2,128)(2,1)S(1)} async-done(((bf16[2,1,256,1024]{3,0,1,2:T(2,128)(2,1)}), bf16[2,1,256,1024]{3,0,1,2:T(2,128)(2,1)S(1)}, u32[]{:S(2)}, u32[]{:S(2)}) %all-to-all-start) | async-done | bytes 1048608 | tf_op jit(solution)/shard_map/all_to_all | solution.py:68
  101.0 0.5 copy.42
  101.5 0.4 copy.45
  101.9 0.7 fusion.24
  102.6 0.3 fusion.5
  102.9 1.6 %convert_element_type.55 = bf16[128,1,4,1,1024]{4,2,0,3,1:T(4,128)(2,1)} reshape(bf16[128,4096]{1,0:T(8,128)(2,1)S(1)} %get-tuple-element.22) | data formatting | bytes 2097152 | tf_op jit(solution)/shard_map/convert_element_type | solution.py:56
  104.5 0.3 pad_maximum_fusion.6
  104.8 1.6 %convert_element_type.56 = bf16[128,1,4,1,1024]{4,2,0,3,1:T(4,128)(2,1)} reshape(bf16[128,4096]{1,0:T(8,128)(2,1)S(1)} %pad_maximum_fusion.6) | data formatting | bytes 2097152 | tf_op jit(solution)/shard_map/convert_element_type | solution.py:57
  (3 shorter events, 0.1 us)
Async XLA Ops:
  0.6 21.9 %copy-start = (bf16[2,1,256,1024]{3,2,1,0:T(8,128)(2,1)S(1)}, bf16[2,1,256,1024]{3,2,1,0:T(8,128)(2,1)}, u32[]{:S(2)}) copy-start(bf16[2,1,256,1024]{3,2,1,0:T(8,128)(2,1)} %param.2) | copy-start | bytes 3145732
  0.6 21.9 %copy-start.1 = (f32[2]{0:T(128)S(1)}, f32[2]{0:T(128)}, u32[]{:S(2)}) copy-start(f32[2]{0:T(128)} %param.3) | copy-start | bytes 28
  1.5 14.0 %collective-permute-start = (f32[2,1,1,1024]{3,2,1,0:T(1,128)S(1)}, f32[2,1,1,1024]{3,2,1,0:T(1,128)S(1)}, u32[]{:S(2)}, u32[]{:S(2)}) collective-permute-start(f32[2,1,1,1024]{3,2,1,0:T(1,128)S(1)} %get-tuple-element.20), channel_id=1, source_target_pairs={{0,1},{1,2},{2,3},{3,4},{4,5},{5,6},{6,7},{8,9},{9,10},{10,11},{11... | collective-permute-start | bytes 24584 | tf_op jit(solution)/shard_map/ppermute | solution.py:17
  12.1 10.4 %collective-permute-start.1 = (f32[2,1,1,1024]{3,2,1,0:T(1,128)S(1)}, f32[2,1,1,1024]{3,2,1,0:T(1,128)S(1)}, u32[]{:S(2)}, u32[]{:S(2)}) collective-permute-start(f32[2,1,1,1024]{3,2,1,0:T(1,128)S(1)} %get-tuple-element.21), channel_id=1, source_target_pairs={{1,0},{2,1},{3,2},{4,3},{5,4},{6,5},{7,6},{9,8},{10,9},{11,10},{12... | collective-permute-start | bytes 24584 | tf_op jit(solution)/shard_map/ppermute | solution.py:18
  25.2 5.3 %collective-permute-start.2 = (f32[2,1,1,1024]{3,2,1,0:T(1,128)S(1)}, f32[2,1,1,1024]{3,2,1,0:T(1,128)S(1)}, u32[]{:S(2)}, u32[]{:S(2)}) collective-permute-start(f32[2,1,1,1024]{3,2,1,0:T(1,128)S(1)} %get-tuple-element.18), channel_id=1, source_target_pairs={{0,1},{1,2},{2,3},{3,4},{4,5},{5,6},{6,7},{8,9},{9,10},{10,11},{11... | collective-permute-start | bytes 24584 | tf_op jit(solution)/shard_map/ppermute | solution.py:17
  27.7 10.4 %collective-permute-start.3 = (f32[2,1,1,1024]{3,2,1,0:T(1,128)S(1)}, f32[2,1,1,1024]{3,2,1,0:T(1,128)S(1)}, u32[]{:S(2)}, u32[]{:S(2)}) collective-permute-start(f32[2,1,1,1024]{3,2,1,0:T(1,128)S(1)} %get-tuple-element.19), channel_id=1, source_target_pairs={{1,0},{2,1},{3,2},{4,3},{5,4},{6,5},{7,6},{9,8},{10,9},{11,10},{12... | collective-permute-start | bytes 24584 | tf_op jit(solution)/shard_map/ppermute | solution.py:18
  40.7 5.3 %collective-permute-start.4 = (f32[2,1,1,1024]{3,2,1,0:T(1,128)S(1)}, f32[2,1,1,1024]{3,2,1,0:T(1,128)S(1)}, u32[]{:S(2)}, u32[]{:S(2)}) collective-permute-start(f32[2,1,1,1024]{3,2,1,0:T(1,128)S(1)} %get-tuple-element.16), channel_id=1, source_target_pairs={{0,1},{1,2},{2,3},{3,4},{4,5},{5,6},{6,7},{8,9},{9,10},{10,11},{11... | collective-permute-start | bytes 24584 | tf_op jit(solution)/shard_map/ppermute | solution.py:17
  42.7 10.4 %collective-permute-start.5 = (f32[2,1,1,1024]{3,2,1,0:T(1,128)S(1)}, f32[2,1,1,1024]{3,2,1,0:T(1,128)S(1)}, u32[]{:S(2)}, u32[]{:S(2)}) collective-permute-start(f32[2,1,1,1024]{3,2,1,0:T(1,128)S(1)} %get-tuple-element.17), channel_id=1, source_target_pairs={{1,0},{2,1},{3,2},{4,3},{5,4},{6,5},{7,6},{9,8},{10,9},{11,10},{12... | collective-permute-start | bytes 24584 | tf_op jit(solution)/shard_map/ppermute | solution.py:18
  57.8 43.1 %all-to-all-start = ((bf16[2,1,256,1024]{3,0,1,2:T(2,128)(2,1)}), bf16[2,1,256,1024]{3,0,1,2:T(2,128)(2,1)S(1)}, u32[]{:S(2)}, u32[]{:S(2)}) async-start(bf16[2,1,256,1024]{3,0,1,2:T(2,128)(2,1)} %copy.41), calls=%async_computation | async-start | bytes 2097152 | tf_op jit(solution)/shard_map/all_to_all | solution.py:68
where the time goes:
time: 107 us; the launch traced here: 106 us
  waiting for transfers between devices  50.3 us (47%)
  starting transfers between devices  37.3 us (35%)
  other arithmetic  10.3 us (10%)
  local copies, waits for them, and re-layouts  7.04 us (7%)
    all_to_all x1, waiting for transfers between devices, local(): lax.all_to_all(stored, 'vol', split_axis=2, concat_axis=0, tiled=True)  28.7 us
    ppermute x3, waiting for transfers between devices, extended_2(): after = lax.ppermute(first, axis, down)  21.6 us
    ppermute x3, starting transfers between devices, extended_2(): before = lax.ppermute(last, axis, up)  14.9 us
    all_to_all x1, starting transfers between devices, local(): lax.all_to_all(stored, 'vol', split_axis=2, concat_axis=0, tiled=True)  14.3 us
    ppermute x3, starting transfers between devices, extended_2(): after = lax.ppermute(first, axis, down)  8.16 us
    add x2, other arithmetic, advance(): return center + 0.2 * total  5.34 us
    convert_element_type x1, other arithmetic, local(): stored = field.astype(jnp.bfloat16)  2.7 us
  transfers between devices with their start and end apart: 7, of which 4 were waited for; matrix products, arithmetic and copies ran while one was open for 1% of the time, Pallas kernels for 0%

commit v1 on v0

--- a/solution.py
+++ b/solution.py
@@ -65,7 +65,12 @@
         extended = extended_2(field, (("strip", 2),), 1)
         field = advance(extended, kap)
     stored = field.astype(jnp.bfloat16)
-    ratio, slope = detrend(lax.all_to_all(stored, "vol", split_axis=2, concat_axis=0, tiled=True))
+    ratio, slope = detrend(
+        jnp.concatenate(
+            lax.all_to_all(jnp.stack(jnp.split(stored, lax.axis_size("vol"), axis=2)), "vol", 0, 0),
+            axis=0,
+        )
+    )
     return (ratio[:, :, :, None, :], slope[:, :, :, None, :])
 
 

time: 107 us -> 146 us (1.36)
  local copies, waits for them, and re-layouts: 7.04 us -> 43.7 us
  other arithmetic: 10.3 us -> 12.9 us
    unnamed x5 -> x68, local copies, waits for them, and re-layouts: 0.39 us -> 39 us
    convert_element_type x1 -> x2, other arithmetic: 2.7 us -> 5.4 us  [local(): stored = field.astype(jnp.bfloat16)]
    convert_element_type x1 -> x0, local copies, waits for them, and re-layouts: 2.05 us -> none  [local(): stored = field.astype(jnp.bfloat16)]
where the time goes in v1:
time: 146 us
  waiting for transfers between devices  50.3 us (34%)
  local copies, waits for them, and re-layouts  43.7 us (30%)
  starting transfers between devices  37.3 us (26%)
  other arithmetic  12.9 us (9%)
    unnamed x68, local copies, waits for them, and re-layouts  39 us
    all_to_all x1, waiting for transfers between devices, local(): lax.all_to_all(jnp.stack(jnp.split(stored, lax.axis_size('vol'), axis=2))...  28.7 us
    ppermute x3, waiting for transfers between devices, extended_2(): after = lax.ppermute(first, axis, down)  21.6 us
    ppermute x3, starting transfers between devices, extended_2(): before = lax.ppermute(last, axis, up)  14.9 us
    all_to_all x1, starting transfers between devices, local(): lax.all_to_all(jnp.stack(jnp.split(stored, lax.axis_size('vol'), axis=2))...  14.3 us
    ppermute x3, starting transfers between devices, extended_2(): after = lax.ppermute(first, axis, down)  8.15 us
    convert_element_type x2, other arithmetic, local(): stored = field.astype(jnp.bfloat16)  5.4 us
    add x2, other arithmetic, advance(): return center + 0.2 * total  5.32 us
  transfers between devices with their start and end apart: 7, of which 4 were waited for; matrix products, arithmetic and copies ran while one was open for 1% of the time, Pallas kernels for 0%

profile of v1, /device:TPU:7, one launch (start us, length us, event | category | flops | bytes accessed | tf_op | source)
XLA Modules:
  0.0 145.8 jit_solution(15673283931357798835)
XLA Ops:
  0.7 0.9 fusion.23
  1.5 10.6 %collective-permute-start = (f32[2,1,1,1024]{3,2,1,0:T(1,128)S(1)}, f32[2,1,1,1024]{3,2,1,0:T(1,128)S(1)}, u32[]{:S(2)}, u32[]{:S(2)}) collective-permute-start(f32[2,1,1,1024]{3,2,1,0:T(1,128)S(1)} %get-tuple-element.12), channel_id=1, source_target_pairs={{0,1},{1,2},{2,3},{3,4},{4,5},{5,6},{6,7},{8,9},{9,10},{10,11},{11... | collective-permute-start | bytes 24584 | tf_op jit(solution)/shard_map/ppermute | solution.py:17
  12.1 1.9 %collective-permute-start.1 = (f32[2,1,1,1024]{3,2,1,0:T(1,128)S(1)}, f32[2,1,1,1024]{3,2,1,0:T(1,128)S(1)}, u32[]{:S(2)}, u32[]{:S(2)}) collective-permute-start(f32[2,1,1,1024]{3,2,1,0:T(1,128)S(1)} %get-tuple-element.13), channel_id=1, source_target_pairs={{1,0},{2,1},{3,2},{4,3},{5,4},{6,5},{7,6},{9,8},{10,9},{11,10},{12... | collective-permute-start | bytes 24584 | tf_op jit(solution)/shard_map/ppermute | solution.py:18
  14.0 1.5 %convert_element_type.49 = f32[2,1,256,1024]{3,2,1,0:T(8,128)S(1)} convert(bf16[2,1,256,1024]{3,2,1,0:T(8,128)(2,1)} %param.2) | non-fusion elementwise | flops 524288 | bytes 3145728 | tf_op jit(solution)/shard_map/convert_element_type | solution.py:63
  15.5 7.0 %collective-permute-done.1 = f32[2,1,1,1024]{3,2,1,0:T(1,128)S(1)} collective-permute-done((f32[2,1,1,1024]{3,2,1,0:T(1,128)S(1)}, f32[2,1,1,1024]{3,2,1,0:T(1,128)S(1)}, u32[]{:S(2)}, u32[]{:S(2)}) %collective-permute-start.1) | collective-permute-done | bytes 8224 | tf_op jit(solution)/shard_map/ppermute | solution.py:18
  22.5 2.7 %convert_add_fusion = f32[2,1,256,1024]{3,2,1,0:T(8,128)S(1)} fusion(bf16[2,1,256,1024]{3,2,1,0:T(8,128)(2,1)S(1)} %copy-done, f32[2,1,256,1024]{3,2,1,0:T(8,128)S(1)} %convert_element_type.49, f32[2,1,1,1024]{3,2,1,0:T(1,128)S(1)} %collective-permute-done.1, f32[2,1,1,1024]{3,2,1,0:T(1,128)S(1)} %collective-permute-done, f32[2]{0:T(128)S(1)} %copy-done.1), kind=kLoop, calls=%fused_computation | loop fusion | flops 14680064 | bytes 5259272 | tf_op jit(solution)/shard_map/add | solution.py:36
  25.2 2.4 %collective-permute-start.2 = (f32[2,1,1,1024]{3,2,1,0:T(1,128)S(1)}, f32[2,1,1,1024]{3,2,1,0:T(1,128)S(1)}, u32[]{:S(2)}, u32[]{:S(2)}) collective-permute-start(f32[2,1,1,1024]{3,2,1,0:T(1,128)S(1)} %get-tuple-element.10), channel_id=1, source_target_pairs={{0,1},{1,2},{2,3},{3,4},{4,5},{5,6},{6,7},{8,9},{9,10},{10,11},{11... | collective-permute-start | bytes 24584 | tf_op jit(solution)/shard_map/ppermute | solution.py:17
  27.6 2.9 %collective-permute-start.3 = (f32[2,1,1,1024]{3,2,1,0:T(1,128)S(1)}, f32[2,1,1,1024]{3,2,1,0:T(1,128)S(1)}, u32[]{:S(2)}, u32[]{:S(2)}) collective-permute-start(f32[2,1,1,1024]{3,2,1,0:T(1,128)S(1)} %get-tuple-element.11), channel_id=1, source_target_pairs={{1,0},{2,1},{3,2},{4,3},{5,4},{6,5},{7,6},{9,8},{10,9},{11,10},{12... | collective-permute-start | bytes 24584 | tf_op jit(solution)/shard_map/ppermute | solution.py:18
  30.5 7.5 %collective-permute-done.3 = f32[2,1,1,1024]{3,2,1,0:T(1,128)S(1)} collective-permute-done((f32[2,1,1,1024]{3,2,1,0:T(1,128)S(1)}, f32[2,1,1,1024]{3,2,1,0:T(1,128)S(1)}, u32[]{:S(2)}, u32[]{:S(2)}) %collective-permute-start.3) | collective-permute-done | bytes 8224 | tf_op jit(solution)/shard_map/ppermute | solution.py:18
  38.1 2.6 %multiply_add_fusion = f32[2,1,256,1024]{3,2,1,0:T(8,128)S(1)} fusion(f32[2,1,256,1024]{3,2,1,0:T(8,128)S(1)} %convert_add_fusion, f32[2,1,1,1024]{3,2,1,0:T(1,128)S(1)} %collective-permute-done.3, f32[2,1,1,1024]{3,2,1,0:T(1,128)S(1)} %collective-permute-done.2, f32[2]{0:T(128)S(1)} %copy-done.1), kind=kLoop, calls=%fused_computation.30 | loop fusion | flops 14155776 | bytes 4210696 | tf_op jit(solution)/shard_map/add | solution.py:36
  40.7 1.9 %collective-permute-start.4 = (f32[2,1,1,1024]{3,2,1,0:T(1,128)S(1)}, f32[2,1,1,1024]{3,2,1,0:T(1,128)S(1)}, u32[]{:S(2)}, u32[]{:S(2)}) collective-permute-start(f32[2,1,1,1024]{3,2,1,0:T(1,128)S(1)} %get-tuple-element.8), channel_id=1, source_target_pairs={{0,1},{1,2},{2,3},{3,4},{4,5},{5,6},{6,7},{8,9},{9,10},{10,11},{11... | collective-permute-start | bytes 24584 | tf_op jit(solution)/shard_map/ppermute | solution.py:17
  42.7 3.4 %collective-permute-start.5 = (f32[2,1,1,1024]{3,2,1,0:T(1,128)S(1)}, f32[2,1,1,1024]{3,2,1,0:T(1,128)S(1)}, u32[]{:S(2)}, u32[]{:S(2)}) collective-permute-start(f32[2,1,1,1024]{3,2,1,0:T(1,128)S(1)} %get-tuple-element.9), channel_id=1, source_target_pairs={{1,0},{2,1},{3,2},{4,3},{5,4},{6,5},{7,6},{9,8},{10,9},{11,10},{12... | collective-permute-start | bytes 24584 | tf_op jit(solution)/shard_map/ppermute | solution.py:18
  46.0 7.0 %collective-permute-done.5 = f32[2,1,1,1024]{3,2,1,0:T(1,128)S(1)} collective-permute-done((f32[2,1,1,1024]{3,2,1,0:T(1,128)S(1)}, f32[2,1,1,1024]{3,2,1,0:T(1,128)S(1)}, u32[]{:S(2)}, u32[]{:S(2)}) %collective-permute-start.5) | collective-permute-done | bytes 8224 | tf_op jit(solution)/shard_map/ppermute | solution.py:18
  53.1 2.7 %fusion.26 = bf16[2,1,256,1024]{3,2,0,1:T(8,128)(2,1)S(1)} fusion(f32[2,1,256,1024]{3,2,1,0:T(8,128)S(1)} %multiply_add_fusion, f32[2,1,1,1024]{3,2,1,0:T(1,128)S(1)} %collective-permute-done.5, f32[2]{0:T(128)S(1)} %copy-done.1, f32[2,1,1,1024]{3,2,1,0:T(1,128)S(1)} %collective-permute-done.4), kind=kLoop, calls=%fused_computation.181 | loop fusion | flops 14680064 | bytes 3162120 | tf_op jit(solution)/shard_map/convert_element_type | solution.py:67
  55.8 0.6 constant_dynamic-update-slice_fusion.63
  56.4 0.6 constant_dynamic-update-slice_fusion.62
  57.0 0.6 constant_dynamic-update-slice_fusion.61
  57.6 0.6 constant_dynamic-update-slice_fusion.60
  58.2 0.6 constant_dynamic-update-slice_fusion.59
  58.8 0.6 constant_dynamic-update-slice_fusion.58
  59.5 0.6 constant_dynamic-update-slice_fusion.57
  60.1 0.6 constant_dynamic-update-slice_fusion.56
  60.7 0.6 constant_dynamic-update-slice_fusion.55
  61.3 0.6 constant_dynamic-update-slice_fusion.54
  61.9 0.6 constant_dynamic-update-slice_fusion.53
  62.5 0.6 constant_dynamic-update-slice_fusion.52
  63.1 0.6 constant_dynamic-update-slice_fusion.51
  63.8 0.6 constant_dynamic-update-slice_fusion.50
  64.4 0.6 constant_dynamic-update-slice_fusion.49
  65.0 0.6 constant_dynamic-update-slice_fusion.48
  65.6 0.6 constant_dynamic-update-slice_fusion.47
  66.2 0.6 constant_dynamic-update-slice_fusion.46
  66.8 0.6 constant_dynamic-update-slice_fusion.45
  67.4 0.6 constant_dynamic-update-slice_fusion.44
  68.7 0.6 constant_dynamic-update-slice_fusion.42
  69.3 0.6 constant_dynamic-update-slice_fusion.41
  69.9 0.6 constant_dynamic-update-slice_fusion.40
  70.5 0.6 constant_dynamic-update-slice_fusion.39
  71.1 0.6 constant_dynamic-update-slice_fusion.38
  72.4 0.6 constant_dynamic-update-slice_fusion.36
  73.6 0.6 constant_dynamic-update-slice_fusion.34
  74.8 0.6 constant_dynamic-update-slice_fusion.32
  76.0 0.6 constant_dynamic-update-slice_fusion.30
  77.3 0.6 constant_dynamic-update-slice_fusion.28
  78.5 0.6 constant_dynamic-update-slice_fusion.26
  79.7 0.6 constant_dynamic-update-slice_fusion.24
  81.0 0.6 constant_dynamic-update-slice_fusion.22
  82.2 0.6 constant_dynamic-update-slice_fusion.20
  83.4 0.6 constant_dynamic-update-slice_fusion.18
  84.6 0.6 constant_dynamic-update-slice_fusion.16
  85.9 0.6 constant_dynamic-update-slice_fusion.14
  87.1 0.6 constant_dynamic-update-slice_fusion.12
  88.3 0.6 constant_dynamic-update-slice_fusion.10
  89.6 0.6 constant_dynamic-update-slice_fusion.8
  90.8 0.6 constant_dynamic-update-slice_fusion.6
  92.0 0.6 constant_dynamic-update-slice_fusion.4
  93.2 0.6 constant_dynamic-update-slice_fusion.2
  94.5 2.7 %add_convert_fusion = bf16[2,1,256,1024]{3,2,1,0:T(8,128)(2,1)S(1)} fusion(f32[2,1,256,1024]{3,2,1,0:T(8,128)S(1)} %multiply_add_fusion, f32[2,1,1,1024]{3,2,1,0:T(1,128)S(1)} %collective-permute-done.5, f32[2,1,1,1024]{3,2,1,0:T(1,128)S(1)} %collective-permute-done.4, f32[2]{0:T(128)S(1)} %copy-done.1), kind=kLoop, calls=%fused_computation.29 | loop fusion | flops 14680064 | bytes 3162120 | tf_op jit(solution)/shard_map/convert_element_type | solution.py:67
  97.2 0.6 constant_dynamic-update-slice_fusion
  97.8 14.3 %all-to-all-start = ((bf16[64,2,1,4,1024]{4,3,1,2,0:T(4,128)(2,1)}), bf16[64,2,1,4,1024]{4,3,1,2,0:T(4,128)(2,1)S(1)}, u32[]{:S(2)}, u32[]{:S(2)}) async-start(bf16[64,2,1,4,1024]{4,3,1,2,0:T(4,128)(2,1)} %constant_dynamic-update-slice_fusion), calls=%async_computation | async-start | bytes 2097152 | tf_op jit(solution)/shard_map/all_to_all | solution.py:70
  112.2 28.7 %all-to-all-done = bf16[64,2,1,4,1024]{4,3,1,2,0:T(4,128)(2,1)S(1)} async-done(((bf16[64,2,1,4,1024]{4,3,1,2,0:T(4,128)(2,1)}), bf16[64,2,1,4,1024]{4,3,1,2,0:T(4,128)(2,1)S(1)}, u32[]{:S(2)}, u32[]{:S(2)}) %all-to-all-start) | async-done | bytes 1048608 | tf_op jit(solution)/shard_map/all_to_all | solution.py:70
  141.3 0.6 fusion.24
  142.3 1.6 %convert_element_type.55 = bf16[128,1,4,1,1024]{4,2,0,3,1:T(4,128)(2,1)} reshape(bf16[128,4096]{1,0:T(8,128)(2,1)S(1)} %get-tuple-element.14) | data formatting | bytes 2097152 | tf_op jit(solution)/shard_map/convert_element_type | solution.py:56
  144.2 1.6 %convert_element_type.56 = bf16[128,1,4,1,1024]{4,2,0,3,1:T(4,128)(2,1)} reshape(bf16[128,4096]{1,0:T(8,128)(2,1)S(1)} %pad_maximum_fusion.6) | data formatting | bytes 2097152 | tf_op jit(solution)/shard_map/convert_element_type | solution.py:57
  (34 shorter events, 13.4 us)
Async XLA Ops:
  0.6 21.9 %copy-start = (bf16[2,1,256,1024]{3,2,1,0:T(8,128)(2,1)S(1)}, bf16[2,1,256,1024]{3,2,1,0:T(8,128)(2,1)}, u32[]{:S(2)}) copy-start(bf16[2,1,256,1024]{3,2,1,0:T(8,128)(2,1)} %param.2) | copy-start | bytes 3145732
  0.6 21.9 %copy-start.1 = (f32[2]{0:T(128)S(1)}, f32[2]{0:T(128)}, u32[]{:S(2)}) copy-start(f32[2]{0:T(128)} %param.3) | copy-start | bytes 28
  1.5 14.0 %collective-permute-start = (f32[2,1,1,1024]{3,2,1,0:T(1,128)S(1)}, f32[2,1,1,1024]{3,2,1,0:T(1,128)S(1)}, u32[]{:S(2)}, u32[]{:S(2)}) collective-permute-start(f32[2,1,1,1024]{3,2,1,0:T(1,128)S(1)} %get-tuple-element.12), channel_id=1, source_target_pairs={{0,1},{1,2},{2,3},{3,4},{4,5},{5,6},{6,7},{8,9},{9,10},{10,11},{11... | collective-permute-start | bytes 24584 | tf_op jit(solution)/shard_map/ppermute | solution.py:17
  12.1 10.4 %collective-permute-start.1 = (f32[2,1,1,1024]{3,2,1,0:T(1,128)S(1)}, f32[2,1,1,1024]{3,2,1,0:T(1,128)S(1)}, u32[]{:S(2)}, u32[]{:S(2)}) collective-permute-start(f32[2,1,1,1024]{3,2,1,0:T(1,128)S(1)} %get-tuple-element.13), channel_id=1, source_target_pairs={{1,0},{2,1},{3,2},{4,3},{5,4},{6,5},{7,6},{9,8},{10,9},{11,10},{12... | collective-permute-start | bytes 24584 | tf_op jit(solution)/shard_map/ppermute | solution.py:18
  25.2 5.3 %collective-permute-start.2 = (f32[2,1,1,1024]{3,2,1,0:T(1,128)S(1)}, f32[2,1,1,1024]{3,2,1,0:T(1,128)S(1)}, u32[]{:S(2)}, u32[]{:S(2)}) collective-permute-start(f32[2,1,1,1024]{3,2,1,0:T(1,128)S(1)} %get-tuple-element.10), channel_id=1, source_target_pairs={{0,1},{1,2},{2,3},{3,4},{4,5},{5,6},{6,7},{8,9},{9,10},{10,11},{11... | collective-permute-start | bytes 24584 | tf_op jit(solution)/shard_map/ppermute | solution.py:17
  27.6 10.4 %collective-permute-start.3 = (f32[2,1,1,1024]{3,2,1,0:T(1,128)S(1)}, f32[2,1,1,1024]{3,2,1,0:T(1,128)S(1)}, u32[]{:S(2)}, u32[]{:S(2)}) collective-permute-start(f32[2,1,1,1024]{3,2,1,0:T(1,128)S(1)} %get-tuple-element.11), channel_id=1, source_target_pairs={{1,0},{2,1},{3,2},{4,3},{5,4},{6,5},{7,6},{9,8},{10,9},{11,10},{12... | collective-permute-start | bytes 24584 | tf_op jit(solution)/shard_map/ppermute | solution.py:18
  40.7 5.3 %collective-permute-start.4 = (f32[2,1,1,1024]{3,2,1,0:T(1,128)S(1)}, f32[2,1,1,1024]{3,2,1,0:T(1,128)S(1)}, u32[]{:S(2)}, u32[]{:S(2)}) collective-permute-start(f32[2,1,1,1024]{3,2,1,0:T(1,128)S(1)} %get-tuple-element.8), channel_id=1, source_target_pairs={{0,1},{1,2},{2,3},{3,4},{4,5},{5,6},{6,7},{8,9},{9,10},{10,11},{11... | collective-permute-start | bytes 24584 | tf_op jit(solution)/shard_map/ppermute | solution.py:17
  42.7 10.4 %collective-permute-start.5 = (f32[2,1,1,1024]{3,2,1,0:T(1,128)S(1)}, f32[2,1,1,1024]{3,2,1,0:T(1,128)S(1)}, u32[]{:S(2)}, u32[]{:S(2)}) collective-permute-start(f32[2,1,1,1024]{3,2,1,0:T(1,128)S(1)} %get-tuple-element.9), channel_id=1, source_target_pairs={{1,0},{2,1},{3,2},{4,3},{5,4},{6,5},{7,6},{9,8},{10,9},{11,10},{12... | collective-permute-start | bytes 24584 | tf_op jit(solution)/shard_map/ppermute | solution.py:18
  97.8 43.1 %all-to-all-start = ((bf16[64,2,1,4,1024]{4,3,1,2,0:T(4,128)(2,1)}), bf16[64,2,1,4,1024]{4,3,1,2,0:T(4,128)(2,1)S(1)}, u32[]{:S(2)}, u32[]{:S(2)}) async-start(bf16[64,2,1,4,1024]{4,3,1,2,0:T(4,128)(2,1)} %constant_dynamic-update-slice_fusion), calls=%async_computation | async-start | bytes 2097152 | tf_op jit(solution)/shard_map/all_to_all | solution.py:70
